TPU v7x, 128 devices: a whole 4x4x4 slice. The times are simulated.
128 devices in a mesh: rows: 8 (over z, core), cache: 16 (over x, y).
Axes of the slice: x: 4, y: 4, z: 4, core: 2. Of those that a mesh axis runs over, the one named last changes fastest.
Arguments:
- queries: bfloat16 [32, 128, 576], P('rows', 'cache'), may hold values from -20 to 20
- prefix_cache: bfloat16 [256, 1024, 576], P(('rows', 'cache')), may hold values from -12 to 12
- suffix_cache: bfloat16 [32, 1024, 576], P('rows'), may hold values from -12 to 12
- suffix_len: int32 [32], P('rows'), may hold values from 2 to 1024, as said below
- touch_mask: int32 [32, 256], replicated, may hold values from 0 to 1, as said below
- block_slot: int32 [256], replicated, may hold values from 0 to 255, as said below
Outputs:
- latent_out: bfloat16 [32, 128, 512], P('rows', 'cache')
- lse_out: float32 [32, 128], P('rows', 'cache')
Inputs may be any that keep to these rules, and one draw needn't show every extreme that they name: `suffix_len`: some request has exactly 1024 suffix tokens. `touch_mask`: each request touches 4 to 16 logical blocks; some request touches exactly 4 and some exactly 16. Within each aligned block of 4 requests, at most 2 requests read blocks held by any one holder, and in every such block some holder is read by exactly 2 of them. `block_slot`: each slot holds exactly one logical block.
All inputs are finite; a program needn't handle non-finite values.
Results may differ from a plain program's by a relative error of at most 0.0048.
Values may be sent and summed in bfloat16 or wider, within the bound.
No kernel may reach another device: no remote copies, remote signals or barrier semaphores. Data moves between devices by JAX's collectives and lax.ppermute only.
A program may use at most 64 MiB of HBM per device.

v0:
```python
import jax
import jax.numpy as jnp
from jax import lax
from jax.sharding import PartitionSpec as P

H = 128
LAT = 512
DK = 576
BLK = 1024
BLK_DEV = 2
SUF = 1024


SOFTMAX_SCALE = 192.0 ** (-0.5)
MASKED_SCORE = -1e30


def combine(parts_out, parts_lse, suffix_out, suffix_lse):
    ceiling = jnp.maximum(jnp.max(parts_lse, axis=0), suffix_lse)
    part_weight = jnp.exp(parts_lse - ceiling[None])
    suffix_weight = jnp.exp(suffix_lse - ceiling)
    merged_total = suffix_weight + jnp.sum(part_weight, axis=0)
    merged = suffix_weight[..., None] * suffix_out + jnp.sum(
        part_weight[..., None] * parts_out.astype(jnp.float32), axis=0
    )
    return (
        (merged / merged_total[..., None]).astype(jnp.bfloat16),
        ceiling + jnp.log(merged_total),
    )


def on_device(queries, prefix_cache, suffix_cache, suffix_len, touch_mask, block_slot):
    panel_rows = queries.shape[0]
    cache_size = lax.axis_size("cache")
    slot_first = (lax.axis_index("rows") * cache_size + lax.axis_index("cache")) * BLK_DEV
    local_slots = slot_first + jnp.arange(BLK_DEV, dtype=jnp.int32)
    matches = (block_slot[:, None] == local_slots[None, :]).astype(jnp.float32)
    slot_touch = jnp.dot(touch_mask.astype(jnp.float32), matches)
    key_rows = prefix_cache.reshape(BLK_DEV * BLK, DK)
    value_rows = key_rows[:, :LAT]

    def holder_part(query_block, touch_block):
        block_rows = query_block.shape[0]
        head_count = query_block.shape[1]
        flat_rows = query_block.reshape(block_rows * head_count, DK)
        scores = lax.dot_general(
            flat_rows, key_rows, (((1,), (1,)), ((), ())), preferred_element_type=jnp.float32
        )
        scores = (scores * SOFTMAX_SCALE).reshape(block_rows, head_count, BLK_DEV * BLK)
        live_keys = jnp.repeat(touch_block > 0.5, BLK, axis=1)[:, None, :]
        scores = jnp.where(live_keys, scores, MASKED_SCORE)
        row_max = jnp.max(scores, axis=2)
        exponent = jnp.exp(scores - row_max[..., None])
        totals = jnp.sum(exponent, axis=2)
        weights = exponent.astype(jnp.bfloat16).reshape(block_rows * head_count, BLK_DEV * BLK)
        partial_value = jnp.dot(weights, value_rows, preferred_element_type=jnp.float32).reshape(
            block_rows, head_count, LAT
        )
        partial_value = partial_value / totals[..., None]
        touched = jnp.sum(touch_block, axis=1) > 0.5
        block_out = jnp.where(touched[:, None, None], partial_value, 0.0).astype(jnp.bfloat16)
        block_lse = jnp.where(touched[:, None], row_max + jnp.log(totals), MASKED_SCORE)
        return (block_out, block_lse)

    query_panel = lax.all_gather(queries, "cache", axis=1, tiled=True)
    panel_piece = lax.all_gather(query_panel, "rows", axis=0, tiled=True)
    piece_rows = panel_piece.shape[0]
    groups = piece_rows // panel_rows

    def grouped(block_pair):
        return holder_part(block_pair[0], block_pair[1])

    piece_out, piece_lse = lax.map(
        grouped,
        (
            panel_piece.reshape(groups, panel_rows, H, DK),
            slot_touch.reshape(groups, panel_rows, BLK_DEV),
        ),
    )
    piece_out = piece_out.reshape(piece_rows, H, LAT)
    piece_lse = piece_lse.reshape(piece_rows, H)
    parts_out, parts_lse = (
        lax.all_to_all(
            lax.all_to_all(
                piece_out[None].astype(jnp.float32), "rows", split_axis=1, concat_axis=0, tiled=True
            ),
            "cache",
            split_axis=2,
            concat_axis=0,
            tiled=True,
        ).astype(jnp.bfloat16),
        lax.all_to_all(
            lax.all_to_all(piece_lse[None], "rows", split_axis=1, concat_axis=0, tiled=True),
            "cache",
            split_axis=2,
            concat_axis=0,
            tiled=True,
        ),
    )
    suffix_scores = (
        jnp.einsum("rhd,rsd->rhs", queries, suffix_cache, preferred_element_type=jnp.float32)
        * SOFTMAX_SCALE
    )
    positions = jnp.arange(SUF, dtype=jnp.int32)
    suffix_live = (positions[None, :] < suffix_len[:, None])[:, None, :]
    suffix_scores = jnp.where(suffix_live, suffix_scores, MASKED_SCORE)
    suffix_max = jnp.max(suffix_scores, axis=2)
    suffix_exponent = jnp.exp(suffix_scores - suffix_max[..., None])
    suffix_total = jnp.sum(suffix_exponent, axis=2)
    suffix_weights = suffix_exponent.astype(jnp.bfloat16)
    suffix_out = jnp.einsum(
        "rhs,rsl->rhl", suffix_weights, suffix_cache[:, :, :LAT], preferred_element_type=jnp.float32
    )
    suffix_out = suffix_out / suffix_total[..., None]
    suffix_lse = suffix_max + jnp.log(suffix_total)
    latent_out, lse_out = combine(parts_out, parts_lse, suffix_out, suffix_lse)
    return (latent_out, lse_out)


def solution(mesh):
    in_specs = (
        P("rows", "cache", None),
        P(("rows", "cache"), None, None),
        P("rows", None, None),
        P("rows"),
        P(),
        P(),
    )
    out_specs = (P("rows", "cache", None), P("rows", "cache"))
    return jax.shard_map(
        on_device, mesh=mesh, in_specs=in_specs, out_specs=out_specs, check_vma=False
    )
```

profile of v0, /device:TPU:0, one launch (start us, length us, event | category | flops | bytes accessed | tf_op | source)
XLA Modules:
  0.0 296.6 jit_solution(16826584185083079673)
XLA Ops:
  7.2 0.8 copy.33
  8.0 24.5 %all_gather.6 = bf16[4,128,576]{2,0,1:T(4,128)(2,1)S(1)} all-gather(bf16[4,8,576]{2,0,1:T(4,128)(2,1)S(1)} %copy.33), channel_id=1, replica_groups=mesh['rows'=8,'cache'=16] {'cache'}, dimensions={1}, use_global_device_ids=true | all-gather | bytes 626688 | tf_op jit(solution)/shard_map/all_gather | solution.py:65
  32.5 1.3 copy.34
  33.9 1.0 convolution_bitcast_fusion
  35.0 3.1 %copy.35 = bf16[2,1024,576]{2,1,0:T(8,128)(2,1)S(1)} copy(bf16[2,1024,576]{1,2,0:T(8,128)(2,1)} %param.9) | data formatting | bytes 4718592 | tf_op args[1]
  38.1 1.5 slice.8
  39.7 29.2 %all-gather.2.cloned.1.call-done = bf16[32,128,576]{1,2,0:T(8,128)(2,1)} async-done(((bf16[4,128,576]{1,2,0:T(8,128)(2,1)}), bf16[32,128,576]{1,2,0:T(8,128)(2,1)}) %all-gather.2.cloned.1.call-update) | async-done | bytes 4718608 | tf_op jit(solution)/shard_map/all_gather | solution.py:66
  68.9 73.9 %while.12 = (s32[]{:T(128)}, bf16[8,4,128,512]{3,2,1,0:T(8,128)(2,1)}, f32[8,4,128]{2,1,0:T(4,128)S(1)}, f32[8,4,2]{2,1,0:T(4,128)S(1)}, bf16[8,4,128,576]{2,3,1...) while((s32[]{:T(128)}, bf16[8,4,128,512]{3,2,1,0:T(8,128)(2,1)}, ...), condition=%wide.region_6.7_spmd, body=%wide.region_2.6_spmd.sunk | while | flops 2290876416 | bytes 28941076 | solution.py:73
  69.1 1.9 constant_dynamic-slice_fusion.2
  71.0 1.4 copy.52
  72.4 2.0 fusion.70
  74.4 1.1 fusion.71
  76.0 2.1 fusion.72
  78.3 1.9 constant_dynamic-slice_fusion.2
  80.2 1.4 copy.52
  81.6 2.0 fusion.70
  83.6 1.1 fusion.71
  85.2 2.1 fusion.72
  87.5 1.9 constant_dynamic-slice_fusion.2
  89.5 1.4 copy.52
  90.8 2.0 fusion.70
  92.9 1.1 fusion.71
  94.5 2.1 fusion.72
  96.8 1.9 constant_dynamic-slice_fusion.2
  98.7 1.4 copy.52
  100.1 2.0 fusion.70
  102.1 1.1 fusion.71
  103.3 0.4 copy-done
  103.7 2.1 fusion.72
  106.0 1.9 constant_dynamic-slice_fusion.2
  108.0 1.4 copy.52
  109.3 2.0 fusion.70
  111.3 1.1 fusion.71
  112.9 2.1 fusion.72
  115.3 1.9 constant_dynamic-slice_fusion.2
  117.2 1.4 copy.52
  118.6 2.0 fusion.70
  120.6 1.1 fusion.71
  122.2 2.0 fusion.72
  124.5 1.9 constant_dynamic-slice_fusion.2
  126.4 1.4 copy.52
  127.8 2.0 fusion.70
  129.8 1.1 fusion.71
  131.4 2.1 fusion.72
  133.7 1.9 constant_dynamic-slice_fusion.2
  135.7 1.4 copy.52
  137.0 2.0 fusion.70
  139.0 1.1 fusion.71
  140.6 2.1 fusion.72
  142.8 8.1 %all_to_all.48 = f32[1,32,128]{2,0,1:T(1,128)S(1)} all-to-all(f32[1,32,128]{2,0,1:T(1,128)S(1)} %bitcast.110), channel_id=1, replica_groups=mesh['rows'=8,'cache'=16] {'rows'}, dimensions={1} | all-to-all | bytes 32768 | tf_op jit(solution)/shard_map/all_to_all | solution.py:93
  151.0 4.5 %all-to-all-start.2 = ((bf16[1,32,128,512]{3,2,0,1:T(8,128)(2,1)}), bf16[1,32,128,512]{3,2,0,1:T(8,128)(2,1)}, u32[]{:S(2)}, u32[]{:S(2)}) async-start(bf16[1,32,128,512]{3,2,0,1:T(8,128)(2,1)} %bitcast.101), calls=%async_computation.2 | async-start | bytes 8388608 | tf_op jit(solution)/shard_map/all_to_all | solution.py:84
  155.7 0.9 reshape.179
  156.5 48.6 %all-to-all-done.2 = bf16[1,32,128,512]{3,2,0,1:T(8,128)(2,1)} async-done(((bf16[1,32,128,512]{3,2,0,1:T(8,128)(2,1)}), bf16[1,32,128,512]{3,2,0,1:T(8,128)(2,1)}, u32[]{:S(2)}, u32[]{:S(2)}) %all-to-all-start.2) | async-done | bytes 4194336 | tf_op jit(solution)/shard_map/all_to_all | solution.py:84
  205.2 6.8 %all-to-all-start.1 = ((f32[16,1,256]{2,1,0:T(1,128)}), f32[16,1,256]{2,1,0:T(1,128)S(1)}, u32[]{:S(2)}, u32[]{:S(2)}) async-start(f32[16,1,256]{2,1,0:T(1,128)} %reshape.179), calls=%async_computation.1 | async-start | bytes 32768 | tf_op jit(solution)/shard_map/all_to_all | solution.py:92
  212.0 7.4 %copy.42 = bf16[8,4,128,512]{3,1,0,2:T(4,128)(2,1)} copy(bf16[8,4,128,512]{3,2,1,0:T(8,128)(2,1)} %bitcast.18) | data formatting | bytes 8388608 | tf_op jit(solution)/shard_map/all_to_all | solution.py:84
  219.6 7.2 %all-to-all-start.3 = ((bf16[8,4,128,512]{3,1,0,2:T(4,128)(2,1)}), bf16[8,4,128,512]{3,1,0,2:T(4,128)(2,1)}, u32[]{:S(2)}, u32[]{:S(2)}) async-start(bf16[8,4,128,512]{3,1,0,2:T(4,128)(2,1)} %copy.42), calls=%async_computation.3 | async-start | bytes 8388608 | tf_op jit(solution)/shard_map/all_to_all | solution.py:83
  226.9 3.1 %fusion.52 = (f32[4,8]{1,0:T(4,128)S(1)}, f32[4,8,1024]{2,1,0:T(8,128)S(1)}) fusion(bf16[4,8,576]{2,1,0:T(8,128)(2,1)S(1)} %copy-done.1, bf16[4,1024,576]{1,2,0:T(8,128)(2,1)} %param.10, pred[4,1024]{1,0:T(4,128)(4,1)S(1)} %iota_compare_fusion), kind=kOutput, calls=%fused_computation.50 | convolution fusion | flops 37847008 | bytes 4890752 | tf_op jit(solution)/shard_map/rhd,rsd->rhs/dot_general | solution.py:101
  230.3 0.5 broadcast.78
  230.8 0.7 reduce.6
  232.1 0.8 copy.41
  232.9 0.6 log_add_fusion
  233.5 47.7 %all-to-all-done.3 = bf16[8,4,128,512]{3,1,0,2:T(4,128)(2,1)} async-done(((bf16[8,4,128,512]{3,1,0,2:T(4,128)(2,1)}), bf16[8,4,128,512]{3,1,0,2:T(4,128)(2,1)}, u32[]{:S(2)}, u32[]{:S(2)}) %all-to-all-start.3) | async-done | bytes 4194336 | tf_op jit(solution)/shard_map/all_to_all | solution.py:83
  281.3 4.4 %fusion.22 = f32[4,8,512]{2,0,1:T(4,128)S(1)} fusion(bf16[8,4,16,8,512]{4,1,0,3,2:T(4,128)(2,1)} %bitcast.22, f32[16,8,4,8]{2,1,3,0:T(8,128)S(1)} %copy.41), kind=kLoop, calls=%fused_computation.20 | loop fusion | flops 6275072 | bytes 4276224 | tf_op jit(solution)/shard_map/reduce_sum | solution.py:23
  285.7 4.0 %fusion.38 = bf16[4,8,512]{2,1,0:T(8,128)(2,1)} fusion(bf16[4,1024,576]{1,2,0:T(8,128)(2,1)} %param.10, f32[4,8,1024]{2,1,0:T(8,128)S(1)} %get-tuple-element.101, f32[4,8,512]{2,0,1:T(4,128)S(1)} %fusion.22, f32[4,8]{1,0:T(4,128)S(1)} %get-tuple-element.100, f32[4,8]{1,0:T(4,128)S(1)} %get-tuple-element.92, f32[4,8]{1,0:T(4,128)S(1)} %fusion.43, ...), kind=kOutput, calls=%fused_computation.30 | convolution fusion | flops 33701888 | bytes 4424192 | tf_op jit(solution)/shard_map/rhs,rsl->rhl/dot_general | solution.py:111
  (82 shorter events, 7.2 us)
Async XLA Ops:
  7.2 61.7 %all-gather.2.cloned.1.call-start = ((), (), s32[]{:S(2)}) async-start(), calls=%async_computation.4 | async-start | bytes 5308416 | tf_op jit(solution)/shard_map/all_gather | solution.py:66
  74.4 1.6 copy-start
  83.6 1.6 copy-start
  92.9 1.6 copy-start
  102.1 1.6 copy-start
  111.3 1.6 copy-start
  120.6 1.6 copy-start
  129.8 1.6 copy-start
  139.0 1.6 copy-start
  151.0 54.2 %all-to-all-start.2 = ((bf16[1,32,128,512]{3,2,0,1:T(8,128)(2,1)}), bf16[1,32,128,512]{3,2,0,1:T(8,128)(2,1)}, u32[]{:S(2)}, u32[]{:S(2)}) async-start(bf16[1,32,128,512]{3,2,0,1:T(8,128)(2,1)} %bitcast.101), calls=%async_computation.2 | async-start | bytes 8388608 | tf_op jit(solution)/shard_map/all_to_all | solution.py:84
  205.2 14.4 %all-to-all-start.1 = ((f32[16,1,256]{2,1,0:T(1,128)}), f32[16,1,256]{2,1,0:T(1,128)S(1)}, u32[]{:S(2)}, u32[]{:S(2)}) async-start(f32[16,1,256]{2,1,0:T(1,128)} %reshape.179), calls=%async_computation.1 | async-start | bytes 32768 | tf_op jit(solution)/shard_map/all_to_all | solution.py:92
  219.4 7.4 %copy-start.2 = (s32[4]{0:T(128)S(1)}, s32[4]{0:T(128)}, u32[]{:S(2)}) copy-start(s32[4]{0:T(128)} %param.11) | copy-start | bytes 52
  219.4 7.5 %copy-start.1 = (bf16[4,8,576]{2,1,0:T(8,128)(2,1)S(1)}, bf16[4,8,576]{2,1,0:T(8,128)(2,1)}, u32[]{:S(2)}) copy-start(bf16[4,8,576]{2,1,0:T(8,128)(2,1)} %param.8) | copy-start | bytes 110596
  219.6 61.7 %all-to-all-start.3 = ((bf16[8,4,128,512]{3,1,0,2:T(4,128)(2,1)}), bf16[8,4,128,512]{3,1,0,2:T(4,128)(2,1)}, u32[]{:S(2)}, u32[]{:S(2)}) async-start(bf16[8,4,128,512]{3,1,0,2:T(4,128)(2,1)} %copy.42), calls=%async_computation.3 | async-start | bytes 8388608 | tf_op jit(solution)/shard_map/all_to_all | solution.py:83
Sparse Core Ops, SparseCore 0:
  34.0 34.8 all-gather.1
where the time goes:
time: 299 us; the launch traced here: 297 us
  waiting for transfers between devices  126 us (42%)
  local copies, waits for them, and re-layouts  48 us (16%)
  matrix products  40.9 us (14%)
  blocking collectives  32.7 us (11%)
  starting transfers between devices  18.6 us (6%)
  other arithmetic  16.3 us (5%)
  between operations  14.2 us (5%)
    all_to_all x1, waiting for transfers between devices, on_device(): lax.all_to_all(piece_out[None].astype(jnp.float32), 'rows', split_axis=1,...  48.6 us
    all_to_all x1, waiting for transfers between devices, on_device(): lax.all_to_all(lax.all_to_all(piece_out[None].astype(jnp.float32), 'rows'...  47.7 us
    all_gather x1, waiting for transfers between devices, on_device(): panel_piece = lax.all_gather(query_panel, 'rows', axis=0, tiled=True)  29.2 us
    dynamic_slice x16, local copies, waits for them, and re-layouts, on_device(): lax.map(grouped, (panel_piece.reshape(groups, panel_rows, H, DK), slot_to...  26.3 us
    all_gather x1, blocking collectives, on_device(): query_panel = lax.all_gather(queries, 'cache', axis=1, tiled=True)  24.5 us
    dot_general x8, matrix products, holder_part(): jnp.dot(weights, value_rows, preferred_element_type=jnp.float32)  16.5 us
    dot_general x8, matrix products, holder_part(): lax.dot_general(flat_rows, key_rows, (((1,), (1,)), ((), ())), preferred_...  16.2 us
    reduce_sum x8, other arithmetic, holder_part(): totals = jnp.sum(exponent, axis=2)  8.62 us
  transfers between devices with their start and end apart: 4, of which 4 were waited for; matrix products, arithmetic and copies ran while one was open for 7% of the time, Pallas kernels for 0%

commit v1 on v0

v1 whole, which is shorter than its diff:
```python
import functools
import jax
import jax.numpy as jnp
from jax import lax
from jax.experimental import pallas as pl
from jax.experimental.pallas import tpu as pltpu
from jax.sharding import Mesh, PartitionSpec as P

H = 128
LAT = 512
DK = 576
BLK = 1024
BLK_DEV = 2
SUF = 1024
DEVS = 128
ROWS = 8
PACK = 640
GROUPS = 8
GROUP_ROWS = 128

SOFTMAX_SCALE = 192.0 ** (-0.5)
MASKED_SCORE = -1e30
BF = jnp.bfloat16
F32 = jnp.float32
MIB = 1024 * 1024


def iota(shape, dim):
    return lax.broadcasted_iota(jnp.int32, shape, dim)


def ones_where(mask):
    return jnp.where(mask, 1.0, 0.0).astype(BF)


def dot(a, b, ca=1, cb=0):
    return lax.dot_general(a, b, (((ca,), (cb,)), ((), ())), preferred_element_type=F32)


def route_kernel(offset, me_ref, q_ref, touch_ref, slot_ref, send_ref, route_ref, table_ref):
    me = me_ref[0]
    group = lax.shift_right_logical(me, 4)
    n = DEVS * ROWS
    blocks = touch_ref.shape[1]
    onehot = ones_where(iota((blocks, blocks), 0) == slot_ref[...])
    touched = dot(onehot, touch_ref[...].astype(F32).astype(BF), 1, 1)
    touched = touched.astype(BF)
    reqs = touched.shape[1]
    mine = ones_where(iota((reqs, 32), 0) == group * 4 + lax.shift_right_logical(iota((reqs, 32), 1), 3))
    mine_touched = dot(touched, mine).astype(BF)
    row = iota((n, blocks), 0)
    holder = lax.shift_right_logical(iota((n, blocks), 1), 1)
    dev = lax.shift_right_logical(row, 3)
    same_chip = (lax.shift_right_logical(holder, 5) == lax.shift_right_logical(dev, 5)) & (
        (holder & 15) == (dev & 15)
    )
    chip_touch = jnp.minimum(dot(ones_where(same_chip), mine_touched), 1.0)
    earlier = lax.shift_right_logical(iota((32, 32), 0), 3) < lax.shift_right_logical(iota((32, 32), 1), 3)
    earlier = ones_where(earlier & ((iota((32, 32), 0) & 7) == 0))
    rank = dot(chip_touch.astype(BF), earlier)
    row = iota((n, 32), 0)
    slot = (lax.shift_right_logical(row, 2) & 1) + offset
    head = (lax.shift_right_logical(row, 7) & 1) * 4 + (row & 3)
    chosen = (chip_touch > 0.5) & (rank == slot.astype(F32)) & ((iota((n, 32), 1) & 7) == head)
    chosen = ones_where(chosen)
    route_ref[...] = chosen
    send_ref[...] = dot(chosen, q_ref[...]).astype(BF)
    b = iota((8, blocks), 0)
    owner = jnp.where(b < 2, me, me ^ 16)
    wanted = jnp.where(b < 4, owner * 2 + (b & 1), -1)
    block_touch = dot(ones_where(iota((8, blocks), 1) == wanted), touched)
    any_touch = jnp.max(block_touch, axis=0, keepdims=True)
    any_touch = jnp.broadcast_to(any_touch, (8, reqs))
    before = (lax.shift_right_logical(iota((reqs, reqs), 0), 2) == lax.shift_right_logical(iota((reqs, reqs), 1), 2)) & (
        iota((reqs, reqs), 0) < iota((reqs, reqs), 1)
    )
    place = dot(any_touch.astype(BF), ones_where(before))
    in_group = ones_where(lax.shift_right_logical(iota((reqs, 128), 0), 2) == iota((reqs, 128), 1))
    first = dot(jnp.where(place == float(offset), block_touch, 0.0).astype(BF), in_group)
    second = dot(jnp.where(place == float(offset + 1), block_touch, 0.0).astype(BF), in_group)
    chip = iota((64, blocks), 0)
    holder = lax.shift_right_logical(iota((64, blocks), 1), 1)
    of_chip = (lax.shift_right_logical(holder, 5) == lax.shift_right_logical(chip, 4)) & (
        (holder & 15) == (chip & 15)
    )
    on_chip = jnp.minimum(dot(ones_where(of_chip), touched), 1.0).astype(BF)
    most = jnp.max(jnp.max(dot(on_chip, in_group), axis=0, keepdims=True), axis=1, keepdims=True)
    bits = (first + 2.0 * second).astype(jnp.int32)
    table_ref[...] = jnp.where(iota((8, 128), 0) == 7, most.astype(jnp.int32), bits)


def route(offset, me, q_rows, touch_mask, block_slot):
    n = DEVS * ROWS
    vmem = pl.BlockSpec(memory_space=pltpu.VMEM)
    return pl.pallas_call(
        functools.partial(route_kernel, offset),
        out_shape=(
            jax.ShapeDtypeStruct((n, DK), BF),
            jax.ShapeDtypeStruct((n, 32), BF),
            jax.ShapeDtypeStruct((8, 128), jnp.int32),
        ),
        in_specs=[pl.BlockSpec(memory_space=pltpu.SMEM), vmem, vmem, vmem],
        out_specs=(vmem, vmem, vmem),
        compiler_params=pltpu.CompilerParams(vmem_limit_bytes=32 * MIB),
        cost_estimate=pl.CostEstimate(flops=2 * n * 32 * 1024, bytes_accessed=2 * n * DK, transcendentals=0),
        name="route",
    )(me, q_rows, touch_mask, block_slot.reshape(1, -1))


def holder_kernel(table_ref, q_ref, own_ref, peer_ref, out_ref, keys, top, total, acc, sems):
    copies = []
    for b in range(4):
        src = own_ref if b < 2 else peer_ref
        copies.append(pltpu.make_async_copy(src.at[b & 1], keys.at[b], sems.at[b]))
        copies[-1].start()
    top[...] = jnp.full(top.shape, MASKED_SCORE, F32)
    total[...] = jnp.ones(total.shape, F32)
    acc[...] = jnp.zeros(acc.shape, F32)
    for b in range(4):
        copies[b].wait()

        def step(g, carry, b=b):
            bits = table_ref[b, g]

            @pl.when(bits > 0)
            def _():
                s = dot(q_ref[g], keys[b], 1, 1) * SOFTMAX_SCALE
                second = (lax.shift_right_logical(iota((GROUP_ROWS, 1), 0), 2) & 1) == 1
                live = jnp.where(second, lax.shift_right_logical(bits, 1), bits & 1) > 0
                s = jnp.where(live, s, MASKED_SCORE)
                old = top[g]
                new = jnp.maximum(old, jnp.max(s, axis=1, keepdims=True))
                scale = jnp.exp(old - new)
                p = jnp.exp(s - new)
                top[g] = new
                total[g] = total[g] * scale + jnp.sum(p, axis=1, keepdims=True)
                acc[g] = acc[g] * scale + dot(p.astype(BF), keys[b, :, :LAT])

            return carry

        lax.fori_loop(0, GROUPS, step, 0)

    def finish(g, carry):
        out_ref[g, :, :LAT] = (acc[g] / total[g]).astype(BF)
        lse = top[g] + jnp.log(total[g])
        high = lse.astype(BF).astype(F32)
        middle = (lse - high).astype(BF).astype(F32)
        low = lse - high - middle
        lane = iota((GROUP_ROWS, PACK - LAT), 1)
        tail = jnp.where(lane == 0, high, 0.0)
        tail = jnp.where(lane == 1, middle, tail)
        tail = jnp.where(lane == 2, low, tail)
        tail = jnp.where(lane == 3, 1.0, tail)
        out_ref[g, :, LAT:] = tail.astype(BF)
        return carry

    lax.fori_loop(0, GROUPS, finish, 0)


def holder(table, queries, own, peer):
    return pl.pallas_call(
        holder_kernel,
        out_shape=jax.ShapeDtypeStruct((GROUPS, GROUP_ROWS, PACK), BF),
        in_specs=[
            pl.BlockSpec(memory_space=pltpu.SMEM),
            pl.BlockSpec(memory_space=pltpu.VMEM),
            pl.BlockSpec(memory_space=pl.ANY),
            pl.BlockSpec(memory_space=pl.ANY),
        ],
        out_specs=pl.BlockSpec(memory_space=pltpu.VMEM),
        scratch_shapes=[
            pltpu.VMEM((4, BLK, DK), BF),
            pltpu.VMEM((GROUPS, GROUP_ROWS, 1), F32),
            pltpu.VMEM((GROUPS, GROUP_ROWS, 1), F32),
            pltpu.VMEM((GROUPS, GROUP_ROWS, LAT), F32),
            pltpu.SemaphoreType.DMA((4,)),
        ],
        compiler_params=pltpu.CompilerParams(vmem_limit_bytes=40 * MIB),
        cost_estimate=pl.CostEstimate(
            flops=2 * 1024 * 1024 * (DK + LAT), bytes_accessed=4 * 2 * BLK * DK, transcendentals=1024 * 1024
        ),
        name="holder",
    )(table, queries, own, peer)


def suffix_kernel(len_ref, q_ref, kv_ref, out_ref, lse_ref):
    r = pl.program_id(0)
    kv = kv_ref[0]
    s = dot(q_ref[0], kv, 1, 1) * SOFTMAX_SCALE
    s = jnp.where(iota(s.shape, 1) < len_ref[r], s, MASKED_SCORE)
    top = jnp.max(s, axis=1, keepdims=True)
    p = jnp.exp(s - top)
    total = jnp.sum(p, axis=1, keepdims=True)
    out_ref[0] = dot(p.astype(BF), kv[:, :LAT]) / total
    lse_ref[0] = jnp.broadcast_to(top + jnp.log(total), lse_ref.shape[1:])


def suffix(lengths, queries, cache):
    reqs, heads, _ = queries.shape
    return pl.pallas_call(
        suffix_kernel,
        grid=(reqs,),
        out_shape=(
            jax.ShapeDtypeStruct((reqs, heads, LAT), F32),
            jax.ShapeDtypeStruct((reqs, heads, 128), F32),
        ),
        in_specs=[
            pl.BlockSpec(memory_space=pltpu.SMEM),
            pl.BlockSpec((1, heads, DK), lambda r: (r, 0, 0)),
            pl.BlockSpec((1, SUF, DK), lambda r: (r, 0, 0)),
        ],
        out_specs=(
            pl.BlockSpec((1, heads, LAT), lambda r: (r, 0, 0)),
            pl.BlockSpec((1, heads, 128), lambda r: (r, 0, 0)),
        ),
        compiler_params=pltpu.CompilerParams(vmem_limit_bytes=32 * MIB),
        cost_estimate=pl.CostEstimate(
            flops=2 * 4 * 256 * 1024 * (DK + LAT), bytes_accessed=4 * 2 * SUF * DK, transcendentals=4 * 8 * 1024
        ),
        name="suffix",
    )(lengths, queries, cache)


def merge_kernel(rounds, *refs):
    parts, routes = refs[:rounds], refs[rounds : 2 * rounds]
    suffix_ref, suffix_lse_ref, out_ref, lse_ref = refs[2 * rounds :]
    heads = 32
    eye = iota((heads, heads), 0) == iota((heads, heads), 1)
    suffix_lse = suffix_lse_ref[:, :1]
    ceiling = jnp.max(jnp.where(eye, suffix_lse, MASKED_SCORE), axis=0, keepdims=True)
    scores = []
    for part, chosen in zip(parts, routes):
        tail = part[:, LAT:].astype(F32)
        lse = tail[:, 0:1] + tail[:, 1:2] + tail[:, 2:3]
        score = jnp.where(chosen[...] > 0.5, lse, MASKED_SCORE)
        scores.append(score)
        ceiling = jnp.maximum(ceiling, jnp.max(score, axis=0, keepdims=True))
    top = jnp.max(jnp.where(eye, ceiling, MASKED_SCORE), axis=1, keepdims=True)
    weight = jnp.exp(suffix_lse - top)
    merged = weight * suffix_ref[...]
    total = weight
    for part, score in zip(parts, scores):
        w = jnp.exp(score - ceiling)
        high = w.astype(BF)
        low = (w - high.astype(F32)).astype(BF)
        both = jnp.concatenate([high, low], axis=1).T
        sums = dot(both, part[...])
        sums = sums[:heads] + sums[heads:]
        merged = merged + sums[:, :LAT]
        total = total + sums[:, LAT + 3 : LAT + 4]
    out_ref[...] = (merged / total).astype(BF)
    lse_ref[...] = jnp.broadcast_to(top + jnp.log(total), lse_ref.shape)


def merge(parts, routes, suffix_out, suffix_lse):
    vmem = pl.BlockSpec(memory_space=pltpu.VMEM)
    out, lse = pl.pallas_call(
        functools.partial(merge_kernel, len(parts)),
        out_shape=(jax.ShapeDtypeStruct((32, LAT), BF), jax.ShapeDtypeStruct((32, 128), F32)),
        in_specs=[vmem] * (2 * len(parts) + 2),
        out_specs=(vmem, vmem),
        compiler_params=pltpu.CompilerParams(vmem_limit_bytes=32 * MIB),
        name="merge",
    )(*parts, *routes, suffix_out, suffix_lse)
    return out, lse[:, 0]


AXES = ("z", "core", "x", "y")


def on_device(queries, prefix_cache, suffix_cache, suffix_len, touch_mask, block_slot):
    reqs, heads, _ = queries.shape
    me = lax.axis_index(AXES).astype(jnp.int32).reshape(1)
    q_rows = queries.reshape(reqs * heads, DK)
    peer = lax.ppermute(prefix_cache, "core", [(0, 1), (1, 0)])

    def one_round(offset, peer):
        send, chosen, table = route(offset, me, q_rows, touch_mask, block_slot)
        got = lax.all_to_all(send.reshape(DEVS, ROWS, DK), AXES, split_axis=0, concat_axis=0, tiled=True)
        parts = holder(table, got.reshape(GROUPS, GROUP_ROWS, DK), prefix_cache, peer)
        parts = lax.all_to_all(parts.reshape(DEVS, ROWS, PACK), AXES, split_axis=0, concat_axis=0, tiled=True)
        return parts.reshape(DEVS * ROWS, PACK), chosen, table

    parts, chosen, table = one_round(0, peer)
    suffix_out, suffix_lse = suffix(suffix_len, queries, suffix_cache)
    suffix_out = suffix_out.reshape(reqs * heads, LAT)
    suffix_lse = suffix_lse.reshape(reqs * heads, 128)

    def one(parts, chosen, peer):
        return merge([parts], [chosen], suffix_out, suffix_lse)

    def two(parts, chosen, peer):
        more, more_chosen, _ = one_round(2, peer)
        return merge([parts, more], [chosen, more_chosen], suffix_out, suffix_lse)

    out, lse = lax.cond(table[7, 0] > 2, two, one, parts, chosen, peer)
    return out.reshape(reqs, heads, LAT), lse.reshape(reqs, heads)


def solution(mesh):
    grid = Mesh(mesh.devices.reshape(4, 2, 4, 4), AXES)
    rows, cache = ("z", "core"), ("x", "y")
    in_specs = (
        P(rows, cache, None),
        P(AXES, None, None),
        P(rows, None, None),
        P(rows),
        P(),
        P(),
    )
    out_specs = (P(rows, cache, None), P(rows, cache))
    return jax.shard_map(
        on_device, mesh=grid, in_specs=in_specs, out_specs=out_specs, check_vma=False
    )
```

time: 299 us -> 85.5 us (0.29)
  waiting for transfers between devices: 126 us -> 20.7 us
  matrix products: 40.9 us -> 0 us
  blocking collectives: 32.7 us -> 0 us
  local copies, waits for them, and re-layouts: 48 us -> 21.8 us
  Pallas kernels: 0 us -> 21.8 us
  other arithmetic: 16.3 us -> 0 us
  between operations: 14.2 us -> 1.39 us
    all_to_all x3 -> x2, waiting for transfers between devices: 96.6 us -> 20.7 us  [the longest x1 13.9 us: one_round(): lax.all_to_all(send.reshape(DEVS, ROWS, DK), AXES, split_axis=0, concat_a...]
    dot_general x19 -> x0, matrix products: 40.9 us -> none  [the longest x8 16.5 us: holder_part(): jnp.dot(weights, value_rows, preferred_element_type=jnp.float32)]
    all_gather x1 -> x0, waiting for transfers between devices: 29.2 us -> none  [on_device(): panel_piece = lax.all_gather(query_panel, 'rows', axis=0, tiled=True)]
    dynamic_slice x16 -> x0, local copies, waits for them, and re-layouts: 26.3 us -> none  [on_device(): lax.map(grouped, (panel_piece.reshape(groups, panel_rows, H, DK), slot_to...]
    all_gather x1 -> x0, blocking collectives: 24.5 us -> none  [on_device(): query_panel = lax.all_gather(queries, 'cache', axis=1, tiled=True)]
    pallas_call x0 -> x4, Pallas kernels: none -> 21.8 us  [the longest x1 13.3 us: holder(): pl.pallas_call(holder_kernel, out_shape=jax.ShapeDtypeStruct((GROUPS, GRO...]
    reduce_sum x19 -> x0, other arithmetic: 14.2 us -> none  [the longest x8 8.62 us: holder_part(): totals = jnp.sum(exponent, axis=2)]
    unnamed x8 -> x18, local copies, waits for them, and re-layouts: 5.09 us -> 16.8 us
  transfers between devices with their start and end apart: 4 -> 3, of which waited for: 4 -> 2; matrix products, arithmetic and copies ran while one was open for 7% -> 19% of each run, Pallas kernels for 0% -> 8%
where the time goes in v1:
time: 85.5 us; the launch traced here: 84.3 us
  Pallas kernels  21.8 us (25%)
  local copies, waits for them, and re-layouts  21.8 us (25%)
  waiting for transfers between devices  20.7 us (24%)
  starting transfers between devices  18.5 us (22%)
  between operations  1.39 us (2%)
    unnamed x18, local copies, waits for them, and re-layouts  16.8 us
    all_to_all x1, waiting for transfers between devices, one_round(): lax.all_to_all(send.reshape(DEVS, ROWS, DK), AXES, split_axis=0, concat_a...  13.9 us
    pallas_call x1, Pallas kernels, holder(): pl.pallas_call(holder_kernel, out_shape=jax.ShapeDtypeStruct((GROUPS, GRO...  13.3 us
    all_to_all x1, starting transfers between devices, one_round(): lax.all_to_all(send.reshape(DEVS, ROWS, DK), AXES, split_axis=0, concat_a...  11.7 us
    all_to_all x1, waiting for transfers between devices, one_round(): lax.all_to_all(parts.reshape(DEVS, ROWS, PACK), AXES, split_axis=0, conca...  6.79 us
    all_to_all x1, starting transfers between devices, one_round(): lax.all_to_all(parts.reshape(DEVS, ROWS, PACK), AXES, split_axis=0, conca...  6.68 us
    ppermute x1, local copies, waits for them, and re-layouts, on_device(): peer = lax.ppermute(prefix_cache, 'core', [(0, 1), (1, 0)])  4.35 us
    pallas_call x1, Pallas kernels, suffix(): pl.pallas_call(suffix_kernel, grid=(reqs,), out_shape=(jax.ShapeDtypeStru...  3.6 us
  transfers between devices with their start and end apart: 3, of which 2 were waited for; matrix products, arithmetic and copies ran while one was open for 19% of the time, Pallas kernels for 8%

profile of v1, /device:TPU:0, one launch (start us, length us, event | category | flops | bytes accessed | tf_op | source)
XLA Modules:
  0.0 84.3 jit_solution(8406151306750512922)
XLA Ops:
  0.6 0.1 collective-permute-start
  0.7 3.2 %route.3 = (bf16[1024,576]{1,0:T(8,128)(2,1)}, bf16[1024,32]{1,0:T(8,128)(2,1)S(1)}, s32[8,128]{1,0:T(8,128)S(1)}) custom-call(s32[1]{0:T(128)} %bitcast.5.me_ref, bf16[32,576]{1,0:T(8,128)(2,1)} %bitcast.25, s32[32,256]{1,0:T(8,128)} %touch_ref.1, s32[1,256]{1,0:T(1,128)} %bitcast.28), custom_call_target="tpu_custom_call" | custom-call | flops 67108864 | bytes 1179648 | tf_op jit(solution)/shard_map/route/pallas_call | solution.py:95
  3.9 11.7 %all-to-all-start.2 = ((bf16[128,8,576]{2,1,0:T(8,128)(2,1)}), bf16[128,8,576]{2,1,0:T(8,128)(2,1)}, u32[]{:S(2)}, u32[]{:S(2)}) async-start(bf16[128,8,576]{2,1,0:T(8,128)(2,1)} %bitcast.9), calls=%async_computation.2 | async-start | bytes 2621440 | tf_op jit(solution)/shard_map/all_to_all | solution.py:279
  15.6 3.1 %copy.16.own_ref = bf16[2,1024,576]{2,1,0:T(8,128)(2,1)S(1)} copy(bf16[2,1024,576]{1,2,0:T(8,128)(2,1)} %param.9) | data formatting | bytes 4718592 | tf_op args[1]
  18.7 0.0 collective-permute-done
  18.7 4.4 %copy.17.peer_ref = bf16[2,1024,576]{2,1,0:T(8,128)(2,1)} copy(bf16[2,1024,576]{1,2,0:T(8,128)(2,1)} %collective-permute-done) | data formatting | bytes 4718592 | tf_op jit(solution)/shard_map/ppermute | solution.py:275
  23.1 13.9 %all-to-all-done.2 = bf16[128,8,576]{2,1,0:T(8,128)(2,1)} async-done(((bf16[128,8,576]{2,1,0:T(8,128)(2,1)}), bf16[128,8,576]{2,1,0:T(8,128)(2,1)}, u32[]{:S(2)}, u32[]{:S(2)}) %all-to-all-start.2) | async-done | bytes 1179680 | tf_op jit(solution)/shard_map/all_to_all | solution.py:279
  37.0 0.0 copy-start.2
  37.0 1.7 %copy-done.2 = bf16[2,1024,576]{2,1,0:T(8,128)(2,1)S(1)} copy-done((bf16[2,1024,576]{2,1,0:T(8,128)(2,1)S(1)}, bf16[2,1024,576]{2,1,0:T(8,128)(2,1)}, u32[]{:S(2)}) %copy-start.2) | copy-done | bytes 2359320
  38.7 13.3 %holder.3 = bf16[8,128,640]{2,1,0:T(8,128)(2,1)S(1)} custom-call(s32[8,128]{1,0:T(8,128)S(1)} %get-tuple-element.59.table_ref, bf16[8,128,576]{2,1,0:T(8,128)(2,1)} %bitcast.10.q_ref, bf16[2,1024,576]{2,1,0:T(8,128)(2,1)S(1)} %copy.16.own_ref, bf16[2,1024,576]{2,1,0:T(8,128)(2,1)S(1)} %copy-done.2), custom_call_target="tpu_custom_call" | custom-call | flops 2281701376 | bytes 4718592 | tf_op jit(solution)/shard_map/holder/pallas_call | solution.py:161
  52.1 0.0 copy-start.3
  52.1 1.2 %copy-done.3 = bf16[8,128,640]{2,1,0:T(8,128)(2,1)} copy-done((bf16[8,128,640]{2,1,0:T(8,128)(2,1)}, bf16[8,128,640]{2,1,0:T(8,128)(2,1)S(1)}, u32[]{:S(2)}) %copy-start.3) | copy-done | bytes 1310744
  53.3 6.7 %all-to-all-start.3 = ((bf16[128,8,640]{2,1,0:T(8,128)(2,1)}), bf16[128,8,640]{2,1,0:T(8,128)(2,1)S(1)}, u32[]{:S(2)}, u32[]{:S(2)}) async-start(bf16[128,8,640]{2,1,0:T(8,128)(2,1)} %bitcast.17), calls=%async_computation.3 | async-start | bytes 2621440 | tf_op jit(solution)/shard_map/all_to_all | solution.py:281
  60.0 0.5 slice.9
  61.1 0.0 copy-start.4
  61.1 0.0 copy-start.8
  61.1 7.7 %copy.18.kv_ref = bf16[4,1024,576]{2,1,0:T(8,128)(2,1)} copy(bf16[4,1024,576]{1,2,0:T(8,128)(2,1)} %param.10) | data formatting | bytes 9437184 | tf_op args[2]
  68.8 0.0 copy-done.4
  68.8 0.0 copy-done.8
  68.8 0.0 copy-start
  68.8 2.5 %copy-done = bf16[4,1024,576]{2,1,0:T(8,128)(2,1)S(1)} copy-done((bf16[4,1024,576]{2,1,0:T(8,128)(2,1)S(1)}, bf16[4,1024,576]{2,1,0:T(8,128)(2,1)}, u32[]{:S(2)}) %copy-start) | copy-done | bytes 4718616
  71.3 0.0 copy-start.9
  71.3 0.0 copy-start.10
  71.3 3.6 %suffix.1 = (f32[4,8,512]{2,1,0:T(8,128)S(1)}, f32[4,8,128]{2,1,0:T(8,128)S(1)}) custom-call(s32[4]{0:T(128)S(1)} %copy-done.4, bf16[4,8,576]{2,1,0:T(8,128)(2,1)S(1)} %copy-done.8, bf16[4,1024,576]{2,1,0:T(8,128)(2,1)S(1)} %copy-done), custom_call_target="tpu_custom_call" | custom-call | flops 2281701376 | bytes 4718592 | tf_op jit(solution)/shard_map/suffix/pallas_call | solution.py:200
  74.9 6.8 %all-to-all-done.3 = bf16[128,8,640]{2,1,0:T(8,128)(2,1)S(1)} async-done(((bf16[128,8,640]{2,1,0:T(8,128)(2,1)}), bf16[128,8,640]{2,1,0:T(8,128)(2,1)S(1)}, u32[]{:S(2)}, u32[]{:S(2)}) %all-to-all-start.3) | async-done | bytes 1310752 | tf_op jit(solution)/shard_map/all_to_all | solution.py:281
  81.7 0.0 copy-done.9
  81.7 0.0 copy-done.10
  81.7 2.0 %conditional.1 = (bf16[32,512]{1,0:T(8,128)(2,1)}, f32[4,8]{1,0:T(4,128)S(1)}) conditional(s32[]{:T(128)} %bitcast.8, (bf16[1024,640]{1,0:T(8,128)(2,1)S(1)}, bf16[1024,32]{1,0:T(8,128)(2,1)S(1)}, f32[32,512]{1,0:T(8,128)S(1)}, f32[32,128]{1,0:T(8,128)S(1)}) %tuple.30, (s32[256]{0:T(256)S(1)}, s32[1]{0:T(128)}, bf16[32,576]{1,0:T(8,128)(2,1)S(1)}, ...), branch_computations={%region_0.0_spmd, %region_1.0_spmd} | conditional | flops 2348810240 | bytes 41681540 | solution.py:296
  81.7 1.7 %merge.2 = (bf16[32,512]{1,0:T(8,128)(2,1)}, f32[32,128]{1,0:T(8,128)S(1)}) custom-call(bf16[1024,640]{1,0:T(8,128)(2,1)S(1)} %get-tuple-element.29.refs_0_, bf16[1024,32]{1,0:T(8,128)(2,1)S(1)} %get-tuple-element.30.refs_1_, f32[32,512]{1,0:T(8,128)S(1)} %get-tuple-element.31.refs_2_, f32[32,128]{1,0:T(8,128)S(1)} %get-tuple-element.32.refs_3_), custom_call_target="tpu_custom_call" | custom-call | tf_op jit(solution)/shard_map/cond/branch_0_fun/merge/pallas_call | solution.py:257
  83.4 0.1 slice_reduce_fusion
  83.5 0.1 reshape.45
  83.8 0.0 copy-start.7
  83.8 0.6 copy-done.7
Async XLA Ops:
  0.6 18.1 %collective-permute-start = (bf16[2,1024,576]{1,2,0:T(8,128)(2,1)}, bf16[2,1024,576]{1,2,0:T(8,128)(2,1)}, u32[]{:S(2)}, u32[]{:S(2)}) collective-permute-start(bf16[2,1024,576]{1,2,0:T(8,128)(2,1)} %param.9), channel_id=1, source_target_pairs={{0,16},{16,0},{1,17},{17,1},{2,18},{18,2},{3,19},{19,3},{4,20},{20... | collective-permute-start | bytes 7077896 | tf_op jit(solution)/shard_map/ppermute | solution.py:275
  3.9 33.1 %all-to-all-start.2 = ((bf16[128,8,576]{2,1,0:T(8,128)(2,1)}), bf16[128,8,576]{2,1,0:T(8,128)(2,1)}, u32[]{:S(2)}, u32[]{:S(2)}) async-start(bf16[128,8,576]{2,1,0:T(8,128)(2,1)} %bitcast.9), calls=%async_computation.2 | async-start | bytes 2621440 | tf_op jit(solution)/shard_map/all_to_all | solution.py:279
  37.0 1.7 %copy-start.2 = (bf16[2,1024,576]{2,1,0:T(8,128)(2,1)S(1)}, bf16[2,1024,576]{2,1,0:T(8,128)(2,1)}, u32[]{:S(2)}) copy-start(bf16[2,1024,576]{2,1,0:T(8,128)(2,1)} %copy.17.peer_ref) | copy-start | bytes 7077892
  52.1 1.2 %copy-start.3 = (bf16[8,128,640]{2,1,0:T(8,128)(2,1)}, bf16[8,128,640]{2,1,0:T(8,128)(2,1)S(1)}, u32[]{:S(2)}) copy-start(bf16[8,128,640]{2,1,0:T(8,128)(2,1)S(1)} %holder.3) | copy-start | bytes 3932164
  53.3 28.5 %all-to-all-start.3 = ((bf16[128,8,640]{2,1,0:T(8,128)(2,1)}), bf16[128,8,640]{2,1,0:T(8,128)(2,1)S(1)}, u32[]{:S(2)}, u32[]{:S(2)}) async-start(bf16[128,8,640]{2,1,0:T(8,128)(2,1)} %bitcast.17), calls=%async_computation.3 | async-start | bytes 2621440 | tf_op jit(solution)/shard_map/all_to_all | solution.py:281
  61.1 7.7 %copy-start.4 = (s32[4]{0:T(128)S(1)}, s32[4]{0:T(128)}, u32[]{:S(2)}) copy-start(s32[4]{0:T(128)} %len_ref.1) | copy-start | bytes 52
  61.1 7.7 %copy-start.8 = (bf16[4,8,576]{2,1,0:T(8,128)(2,1)S(1)}, bf16[4,8,576]{2,1,0:T(8,128)(2,1)}, u32[]{:S(2)}) copy-start(bf16[4,8,576]{2,1,0:T(8,128)(2,1)} %q_ref.1) | copy-start | bytes 110596
  68.8 2.5 %copy-start = (bf16[4,1024,576]{2,1,0:T(8,128)(2,1)S(1)}, bf16[4,1024,576]{2,1,0:T(8,128)(2,1)}, u32[]{:S(2)}) copy-start(bf16[4,1024,576]{2,1,0:T(8,128)(2,1)} %copy.18.kv_ref) | copy-start | bytes 14155780
  71.3 10.4 %copy-start.9 = (s32[32,256]{1,0:T(8,128)S(1)}, s32[32,256]{1,0:T(8,128)}, u32[]{:S(2)}) copy-start(s32[32,256]{1,0:T(8,128)} %touch_ref.1) | copy-start | bytes 98308
  71.3 10.4 %copy-start.10 = (s32[256]{0:T(256)S(1)}, s32[256]{0:T(256)}, u32[]{:S(2)}) copy-start(s32[256]{0:T(256)} %param.13) | copy-start | bytes 3076
  83.8 0.6 copy-start.7
